TPU v7x, 512 devices: a whole 4x8x8 slice. The times are simulated.
512 devices in a mesh: step: 2 (over x_hi), grp: 16 (over y, core), ctx: 16 (over z, x_lo).
Axes of the slice: x: 4 (x_hi: 2, x_lo: 2; x = x_hi * 2 + x_lo), y: 8, z: 8, core: 2. Of those that a mesh axis runs over, the one named last changes fastest.
Arguments:
- queries: bfloat16 [2, 32768, 2560], P('step', ('grp', 'ctx')), parts along dimension 1, may hold values from -22.5 to 22.5
- keys: bfloat16 [2, 32768, 2560], P('step', ('grp', 'ctx')), parts along dimension 1, may hold values from -22.5 to 22.5
- values: bfloat16 [2, 32768, 2560], P('step', ('grp', 'ctx')), parts along dimension 1, may hold values from -6 to 6
- cotangent: bfloat16 [32768, 2560], P(('grp', 'ctx')), parts along dimension 0, may hold values from -6 to 6
- merge_sizes: int32 [32768], P(('grp', 'ctx')), parts along dimension 0, may hold values from 1 to 4
- router_logits: float32 [20], replicated, may hold values from -2 to 2
- gate_plan: int32 [20], replicated, may hold values 0 or 1
Outputs:
- grad_queries: bfloat16 [2, 32768, 2560], P('step', ('grp', 'ctx')), parts along dimension 1
- grad_keys: bfloat16 [2, 32768, 2560], P('step', ('grp', 'ctx')), parts along dimension 1
- grad_values: bfloat16 [2, 32768, 2560], P('step', ('grp', 'ctx')), parts along dimension 1
- router_grad: float32 [320], P('grp'), parts along dimension 0
There are 16 independent parts, one for each index of `grp`. A program takes and returns all parts, laid end to end along the dimension named above; an argument that names none is the same for every part. Nothing has to cross between parts.
All inputs are finite; a program needn't handle non-finite values.
Results may differ from a plain program's by a relative error of at most 0.009.
Values may be sent and summed in bfloat16 or wider, within the bound.
A program may use at most 128 MiB of HBM per device.

v0:
```python
import math

import jax
import jax.numpy as jnp
import numpy as np
from jax import lax
from jax.sharding import PartitionSpec as P

QB = 4


def build_table(devices, head_count, blocks):
    per_device = head_count * blocks // devices
    first_head = [device * per_device // blocks for device in range(devices)]
    last_head = [(device * per_device + per_device - 1) // blocks for device in range(devices)]
    slot_count = max((last_head[device] - first_head[device] + 1 for device in range(devices)))
    table = np.array(
        [
            [min(first_head[device] + slot, head_count - 1) for slot in range(slot_count)]
            for device in range(devices)
        ],
        np.int32,
    )
    valid_mask = np.array(
        [[1.0 for slot in range(slot_count)] for device in range(devices)], np.float32
    )
    return (table, valid_mask, slot_count)


def block_grads(q_block, k_head, v_head, g_block, bias, coef, score_scale):
    scores = (
        lax.dot_general(
            q_block, k_head, (((1,), (1,)), ((), ())), preferred_element_type=jnp.float32
        )
        * score_scale
        + bias[None, :]
    )
    shifted = scores - jnp.max(scores, axis=1, keepdims=True)
    expon = jnp.exp(shifted)
    probs = expon / jnp.sum(expon, axis=1, keepdims=True)
    probs_b = probs.astype(jnp.bfloat16)
    outer = lax.dot_general(
        g_block, v_head, (((1,), (1,)), ((), ())), preferred_element_type=jnp.float32
    )
    rowdot = jnp.sum(probs * outer, axis=1)
    dscore = (coef * probs * (outer - rowdot[:, None])).astype(jnp.bfloat16)
    dq_rows = jnp.dot(dscore, k_head, preferred_element_type=jnp.float32) * score_scale
    dk_part = (
        lax.dot_general(
            dscore, q_block, (((0,), (0,)), ((), ())), preferred_element_type=jnp.float32
        )
        * score_scale
    )
    dv_part = coef * lax.dot_general(
        probs_b, g_block, (((0,), (0,)), ((), ())), preferred_element_type=jnp.float32
    )
    return (dq_rows, dk_part, dv_part, jnp.sum(rowdot))


def body(queries, keys, values, cotangent, merge_sizes, router_logits, gate_plan):
    devices = lax.axis_size("ctx")
    step_index = lax.axis_index("step")
    ctx_index = lax.axis_index("ctx")
    tok_rows = queries.shape[1]
    feature = queries.shape[2]
    head_count = router_logits.shape[0]
    head_size = feature // head_count
    total_rows = tok_rows * devices
    block_rows = total_rows // QB
    score_scale = head_size ** (-0.5)
    per_device = head_count * QB // devices
    full_sizes = lax.all_gather(merge_sizes, "ctx", axis=0, tiled=True)
    bias = jnp.log(full_sizes.astype(jnp.float32))
    beta = jnp.where(gate_plan == 1, jax.nn.sigmoid(router_logits), jnp.float32(1.0))
    weight_step = jnp.where(step_index == 1, beta, 1.0 - beta)
    zero_start = jnp.int32(0)

    def homeward(array):
        return array.reshape(devices, tok_rows, slot_count * head_size)

    table, valid_mask, slot_count = build_table(devices, head_count, QB)
    flat_table = table.reshape(-1)
    table_here = jnp.asarray(table)[ctx_index]
    one_hot = (
        (table[:, :, None] == np.arange(head_count)[None, None, :]) * valid_mask[:, :, None]
    ).astype(np.float32)
    one_hot_all = jnp.asarray(one_hot)

    def outgoing(array):
        picked = jnp.take(array.reshape(tok_rows, head_count, head_size), flat_table, axis=1)
        return picked.reshape(tok_rows, devices, slot_count * head_size)

    def assemble(piece):
        parts = piece.astype(jnp.float32).reshape(devices, tok_rows, slot_count, head_size)
        summed = jnp.einsum("ctsd,csh->thd", parts, one_hot_all, precision=lax.Precision.HIGHEST)
        return summed.reshape(tok_rows, feature).astype(jnp.bfloat16)[None]

    empty = jnp.zeros((total_rows, slot_count, head_size), jnp.float32)
    sent = (outgoing(queries[0]), outgoing(keys[0]), outgoing(values[0]), outgoing(cotangent))
    received = (
        lax.all_to_all(sent[0], "ctx", split_axis=1, concat_axis=0, tiled=True),
        lax.all_to_all(sent[1], "ctx", split_axis=1, concat_axis=0, tiled=True),
        lax.all_to_all(sent[2], "ctx", split_axis=1, concat_axis=0, tiled=True),
        lax.all_to_all(sent[3], "ctx", split_axis=1, concat_axis=0, tiled=True),
    )
    recv_q, recv_k, recv_v, recv_g = [
        piece.reshape(total_rows, slot_count, head_size) for piece in received
    ]

    def locate(unit):
        global_unit = ctx_index * per_device + unit
        head_id = global_unit // QB
        return (head_id - table_here[0], global_unit % QB, head_id)

    def unit_step(unit, carry):
        dq_acc, dk_acc, dv_acc, r_acc = carry
        slot_id, block, head_id = locate(unit)
        start = block * block_rows
        slot_id = slot_id.astype(jnp.int32)
        q_block = lax.dynamic_slice(
            recv_q, (start, slot_id, zero_start), (block_rows, 1, head_size)
        ).reshape(block_rows, head_size)
        g_block = lax.dynamic_slice(
            recv_g, (start, slot_id, zero_start), (block_rows, 1, head_size)
        ).reshape(block_rows, head_size)
        k_head = lax.dynamic_index_in_dim(recv_k, slot_id, 1, keepdims=False)
        v_head = lax.dynamic_index_in_dim(recv_v, slot_id, 1, keepdims=False)
        coef = weight_step[head_id]
        dq_rows, dk_part, dv_part, r_part = block_grads(
            q_block, k_head, v_head, g_block, bias, coef, score_scale
        )
        dq_acc = lax.dynamic_update_slice(dq_acc, dq_rows[:, None, :], (start, slot_id, zero_start))
        dk_old = lax.dynamic_index_in_dim(dk_acc, slot_id, 1, keepdims=True)
        dk_acc = lax.dynamic_update_slice(
            dk_acc, dk_old + dk_part[:, None, :], (zero_start, slot_id, zero_start)
        )
        dv_old = lax.dynamic_index_in_dim(dv_acc, slot_id, 1, keepdims=True)
        dv_acc = lax.dynamic_update_slice(
            dv_acc, dv_old + dv_part[:, None, :], (zero_start, slot_id, zero_start)
        )
        r_acc = r_acc + jnp.where(jnp.arange(slot_count) == slot_id, r_part, jnp.float32(0.0))
        return (dq_acc, dk_acc, dv_acc, r_acc)

    start_carry = (empty, empty, empty, jnp.zeros((slot_count,), jnp.float32))
    dq_acc, dk_acc, dv_acc, r_acc = lax.fori_loop(0, per_device, unit_step, start_carry)
    returned = (
        lax.all_to_all(
            homeward(dq_acc).astype(jnp.bfloat16), "ctx", split_axis=0, concat_axis=0, tiled=True
        ).astype(jnp.float32),
        lax.all_to_all(
            homeward(dk_acc).astype(jnp.bfloat16), "ctx", split_axis=0, concat_axis=0, tiled=True
        ).astype(jnp.float32),
        lax.all_to_all(
            homeward(dv_acc).astype(jnp.bfloat16), "ctx", split_axis=0, concat_axis=0, tiled=True
        ).astype(jnp.float32),
    )
    grad_queries = assemble(returned[0])
    grad_keys = assemble(returned[1])
    grad_values = assemble(returned[2])
    sign_step = jnp.where(step_index == 1, jnp.float32(1.0), jnp.float32(-1.0))
    local_terms = sign_step * jnp.dot(
        r_acc, one_hot_all[ctx_index], precision=lax.Precision.HIGHEST
    )
    total_terms = lax.psum(local_terms, ("step", "ctx"))
    router_grad = beta * (1.0 - beta) * total_terms / math.sqrt(total_rows)
    return (grad_queries, grad_keys, grad_values, router_grad)


def solution(mesh):
    return jax.shard_map(
        body,
        mesh=mesh,
        in_specs=(
            P("step", ("grp", "ctx"), None),
            P("step", ("grp", "ctx"), None),
            P("step", ("grp", "ctx"), None),
            P(("grp", "ctx"), None),
            P(("grp", "ctx")),
            P(),
            P(),
        ),
        out_specs=(
            P("step", ("grp", "ctx"), None),
            P("step", ("grp", "ctx"), None),
            P("step", ("grp", "ctx"), None),
            P("grp"),
        ),
        check_vma=False,
    )
```

profile of v0, /device:TPU:56, one launch (start us, length us, event | category | flops | bytes accessed | tf_op | source)
XLA Modules:
  0.0 415.5 jit_solution(3006667310995166166)
XLA Ops:
  1.3 1.5 copy.76
  5.2 11.3 %all-to-all-start = ((bf16[128,16,256]{0,2,1:T(8,128)(2,1)}), bf16[128,16,256]{0,2,1:T(8,128)(2,1)S(1)}, u32[]{:S(2)}, u32[]{:S(2)}) async-start(bf16[128,16,256]{0,2,1:T(8,128)(2,1)} %bitcast.3), calls=%async_computation | async-start | bytes 2097152 | tf_op jit(solution)/shard_map/all_to_all | solution.py:101
  19.3 25.9 %all-to-all-done = bf16[128,16,256]{0,2,1:T(8,128)(2,1)S(1)} async-done(((bf16[128,16,256]{0,2,1:T(8,128)(2,1)}), bf16[128,16,256]{0,2,1:T(8,128)(2,1)S(1)}, u32[]{:S(2)}, u32[]{:S(2)}) %all-to-all-start) | async-done | bytes 1048608 | tf_op jit(solution)/shard_map/all_to_all | solution.py:101
  45.2 4.3 %all-to-all-start.1 = ((bf16[128,16,256]{0,2,1:T(8,128)(2,1)}), bf16[128,16,256]{0,2,1:T(8,128)(2,1)}, u32[]{:S(2)}, u32[]{:S(2)}) async-start(bf16[128,16,256]{0,2,1:T(8,128)(2,1)} %bitcast.8), calls=%async_computation.1 | async-start | bytes 2097152 | tf_op jit(solution)/shard_map/all_to_all | solution.py:102
  52.3 23.7 %all-to-all-done.1 = bf16[128,16,256]{0,2,1:T(8,128)(2,1)} async-done(((bf16[128,16,256]{0,2,1:T(8,128)(2,1)}), bf16[128,16,256]{0,2,1:T(8,128)(2,1)}, u32[]{:S(2)}, u32[]{:S(2)}) %all-to-all-start.1) | async-done | bytes 1048608 | tf_op jit(solution)/shard_map/all_to_all | solution.py:102
  76.0 4.3 %all-to-all-start.3 = ((bf16[128,16,256]{0,2,1:T(8,128)(2,1)}), bf16[128,16,256]{0,2,1:T(8,128)(2,1)}, u32[]{:S(2)}, u32[]{:S(2)}) async-start(bf16[128,16,256]{0,2,1:T(8,128)(2,1)} %bitcast.20), calls=%async_computation.3 | async-start | bytes 2097152 | tf_op jit(solution)/shard_map/all_to_all | solution.py:103
  83.1 25.3 %all-to-all-done.3 = bf16[128,16,256]{0,2,1:T(8,128)(2,1)} async-done(((bf16[128,16,256]{0,2,1:T(8,128)(2,1)}), bf16[128,16,256]{0,2,1:T(8,128)(2,1)}, u32[]{:S(2)}, u32[]{:S(2)}) %all-to-all-start.3) | async-done | bytes 1048608 | tf_op jit(solution)/shard_map/all_to_all | solution.py:103
  108.4 3.7 all-to-all-start.2
  112.1 49.8 %all-gather = s32[16,1,128]{2,1,0:T(1,128)S(1)} all-gather(s32[1,1,128]{2,1,0:T(1,128)S(1)} %bitcast.211), channel_id=1, replica_groups=mesh['step'=2,'grp'=16,'ctx'=16] {'ctx'}, dimensions={0}, use_global_device_ids=true | all-gather | bytes 8704 | tf_op jit(solution)/shard_map/all_gather | solution.py:72
  165.7 1.9 copy.83
  168.1 1.9 copy.91
  173.2 1.5 broadcast_in_dim.81.clone
  174.9 82.2 %while.22 = (s32[]{:T(128)}, bf16[2048,2,128]{2,0,1:T(8,128)(2,1)}, f32[2048,2,128]{2,0,1:T(8,128)S(1)}, f32[2048,2,128]{2,0,1:T(8,128)}, f32[2]{0:T(128)S(1)}, ...) while((s32[]{:T(128)}, bf16[2048,2,128]{2,0,1:T(8,128)(2,1)}, ...), condition=%wide.region_5.7_spmd.clone, body=%wide.region_0.6_spmd.clone.sunk | while | flops 1371601408 | bytes 63249048 | solution.py:145
  175.6 1.9 fusion.69
  178.4 3.3 fusion.73
  181.7 3.4 multiply_reduce_fusion.3
  185.7 2.4 multiply_convert_fusion.2
  189.5 1.8 fusion.72
  192.0 1.9 fusion.69
  194.9 3.3 fusion.73
  198.2 3.4 multiply_reduce_fusion.3
  202.2 2.4 multiply_convert_fusion.2
  206.0 1.8 fusion.72
  208.5 1.9 fusion.69
  211.3 3.3 fusion.73
  214.6 3.4 multiply_reduce_fusion.3
  218.7 2.4 multiply_convert_fusion.2
  222.4 1.8 fusion.72
  224.9 1.9 fusion.69
  227.8 3.3 fusion.73
  231.1 3.4 multiply_reduce_fusion.3
  235.1 2.4 multiply_convert_fusion.2
  238.9 1.8 fusion.72
  241.4 1.9 fusion.69
  244.2 3.3 fusion.73
  247.5 3.4 multiply_reduce_fusion.3
  251.5 2.4 multiply_convert_fusion.2
  255.3 1.8 fusion.72
  257.1 1.5 copy.96
  260.1 7.3 %all-to-all-start.4 = ((bf16[16,128,256]{1,2,0:T(8,128)(2,1)}), bf16[16,128,256]{1,2,0:T(8,128)(2,1)}, u32[]{:S(2)}, u32[]{:S(2)}) async-start(bf16[16,128,256]{1,2,0:T(8,128)(2,1)} %copy.97), calls=%async_computation.4 | async-start | bytes 2097152 | tf_op jit(solution)/shard_map/all_to_all | solution.py:147
  268.9 1.4 copy.119
  271.6 17.8 %all-to-all-done.4 = bf16[16,128,256]{1,2,0:T(8,128)(2,1)} async-done(((bf16[16,128,256]{1,2,0:T(8,128)(2,1)}), bf16[16,128,256]{1,2,0:T(8,128)(2,1)}, u32[]{:S(2)}, u32[]{:S(2)}) %all-to-all-start.4) | async-done | bytes 1048608 | tf_op jit(solution)/shard_map/all_to_all | solution.py:147
  289.4 4.3 %all-to-all-start.5 = ((bf16[16,128,256]{1,2,0:T(8,128)(2,1)}), bf16[16,128,256]{1,2,0:T(8,128)(2,1)}, u32[]{:S(2)}, u32[]{:S(2)}) async-start(bf16[16,128,256]{1,2,0:T(8,128)(2,1)} %copy.101), calls=%async_computation.5 | async-start | bytes 2097152 | tf_op jit(solution)/shard_map/all_to_all | solution.py:150
  296.0 19.8 %all-to-all-done.5 = bf16[16,128,256]{1,2,0:T(8,128)(2,1)} async-done(((bf16[16,128,256]{1,2,0:T(8,128)(2,1)}), bf16[16,128,256]{1,2,0:T(8,128)(2,1)}, u32[]{:S(2)}, u32[]{:S(2)}) %all-to-all-start.5) | async-done | bytes 1048608 | tf_op jit(solution)/shard_map/all_to_all | solution.py:150
  315.8 3.9 all-to-all-start.6
  320.5 82.3 %psum.7 = f32[20]{0:T(128)S(1)} all-reduce(f32[20]{0:T(128)S(1)} %fusion.38), channel_id=1, replica_groups=mesh['step'=2,'grp'=16,'ctx'=16] {'step','ctx'}, use_global_device_ids=true, to_apply=%region_6.8 | all-reduce | flops 20 | bytes 160 | tf_op jit(solution)/shard_map/psum | solution.py:164
  403.3 1.9 copy.98
  407.7 1.9 copy.102
  (118 shorter events, 52.9 us)
Async XLA Ops:
  1.3 15.3 %copy-start.4 = (bf16[1,128,2560]{2,1,0:T(8,128)(2,1)S(1)}, bf16[1,128,2560]{2,1,0:T(8,128)(2,1)}, u32[]{:S(2)}) copy-start(bf16[1,128,2560]{2,1,0:T(8,128)(2,1)} %param.15) | copy-start | bytes 1966084
  5.2 40.0 %all-to-all-start = ((bf16[128,16,256]{0,2,1:T(8,128)(2,1)}), bf16[128,16,256]{0,2,1:T(8,128)(2,1)S(1)}, u32[]{:S(2)}, u32[]{:S(2)}) async-start(bf16[128,16,256]{0,2,1:T(8,128)(2,1)} %bitcast.3), calls=%async_computation | async-start | bytes 2097152 | tf_op jit(solution)/shard_map/all_to_all | solution.py:101
  16.6 33.0 %copy-start.5 = (bf16[1,128,2560]{2,1,0:T(8,128)(2,1)S(1)}, bf16[1,128,2560]{2,1,0:T(8,128)(2,1)}, u32[]{:S(2)}) copy-start(bf16[1,128,2560]{2,1,0:T(8,128)(2,1)} %param.16) | copy-start | bytes 1966084
  45.2 30.8 %all-to-all-start.1 = ((bf16[128,16,256]{0,2,1:T(8,128)(2,1)}), bf16[128,16,256]{0,2,1:T(8,128)(2,1)}, u32[]{:S(2)}, u32[]{:S(2)}) async-start(bf16[128,16,256]{0,2,1:T(8,128)(2,1)} %bitcast.8), calls=%async_computation.1 | async-start | bytes 2097152 | tf_op jit(solution)/shard_map/all_to_all | solution.py:102
  49.9 30.4 %copy-start.6 = (bf16[128,2560]{1,0:T(8,128)(2,1)S(1)}, bf16[128,2560]{1,0:T(8,128)(2,1)}, u32[]{:S(2)}) copy-start(bf16[128,2560]{1,0:T(8,128)(2,1)} %param.17) | copy-start | bytes 1966084
  76.0 32.4 %all-to-all-start.3 = ((bf16[128,16,256]{0,2,1:T(8,128)(2,1)}), bf16[128,16,256]{0,2,1:T(8,128)(2,1)}, u32[]{:S(2)}, u32[]{:S(2)}) async-start(bf16[128,16,256]{0,2,1:T(8,128)(2,1)} %bitcast.20), calls=%async_computation.3 | async-start | bytes 2097152 | tf_op jit(solution)/shard_map/all_to_all | solution.py:103
  80.4 31.7 %copy-start.8 = (s32[128]{0:T(128)S(1)}, s32[128]{0:T(128)}, u32[]{:S(2)}) copy-start(s32[128]{0:T(128)} %param.18) | copy-start | bytes 1540
  80.4 82.2 %copy-start.9 = (f32[20]{0:T(128)S(1)}, f32[20]{0:T(128)}, u32[]{:S(2)}) copy-start(f32[20]{0:T(128)} %param.19) | copy-start | bytes 244
  80.4 82.2 %copy-start.10 = (s32[20]{0:T(128)S(1)}, s32[20]{0:T(128)}, u32[]{:S(2)}) copy-start(s32[20]{0:T(128)} %param.20) | copy-start | bytes 244
  108.4 62.9 %all-to-all-start.2 = ((bf16[128,16,256]{0,2,1:T(8,128)(2,1)}), bf16[128,16,256]{0,2,1:T(8,128)(2,1)S(1)}, u32[]{:S(2)}, u32[]{:S(2)}) async-start(bf16[128,16,256]{0,2,1:T(8,128)(2,1)} %bitcast.15), calls=%async_computation.2 | async-start | bytes 2097152 | tf_op jit(solution)/shard_map/all_to_all | solution.py:104
  175.5 2.8 copy-start
  178.4 3.3 copy-start.3
  181.7 3.4 copy-start.1
  192.0 2.8 copy-start
  194.9 3.3 copy-start.3
  198.2 3.4 copy-start.1
  208.5 2.8 copy-start
  211.3 3.3 copy-start.3
  214.6 3.4 copy-start.1
  224.9 2.8 copy-start
  227.8 3.3 copy-start.3
  231.1 3.4 copy-start.1
  241.4 2.8 copy-start
  244.2 3.3 copy-start.3
  247.5 3.4 copy-start.1
  260.1 29.3 %all-to-all-start.4 = ((bf16[16,128,256]{1,2,0:T(8,128)(2,1)}), bf16[16,128,256]{1,2,0:T(8,128)(2,1)}, u32[]{:S(2)}, u32[]{:S(2)}) async-start(bf16[16,128,256]{1,2,0:T(8,128)(2,1)} %copy.97), calls=%async_computation.4 | async-start | bytes 2097152 | tf_op jit(solution)/shard_map/all_to_all | solution.py:147
  267.6 26.2 %copy-start.2 = (f32[2048,2,128]{2,0,1:T(8,128)S(1)}, f32[2048,2,128]{2,0,1:T(8,128)}, u32[]{:S(2)}) copy-start(f32[2048,2,128]{2,0,1:T(8,128)} %get-tuple-element.323) | copy-start | bytes 6291460
  289.4 26.3 %all-to-all-start.5 = ((bf16[16,128,256]{1,2,0:T(8,128)(2,1)}), bf16[16,128,256]{1,2,0:T(8,128)(2,1)}, u32[]{:S(2)}, u32[]{:S(2)}) async-start(bf16[16,128,256]{1,2,0:T(8,128)(2,1)} %copy.101), calls=%async_computation.5 | async-start | bytes 2097152 | tf_op jit(solution)/shard_map/all_to_all | solution.py:150
  294.5 110.8 %copy-start.7 = (f32[16,2,20,1]{2,0,1,3:T(8,128)S(1)}, f32[16,2,20,1]{2,0,1,3:T(8,128)}, u32[]{:S(2)}) copy-start(f32[16,2,20,1]{2,0,1,3:T(8,128)} %constant.245) | copy-start | bytes 7684
  315.8 96.3 %all-to-all-start.6 = ((bf16[16,128,256]{1,2,0:T(8,128)(2,1)}), bf16[16,128,256]{1,2,0:T(8,128)(2,1)S(1)}, u32[]{:S(2)}, u32[]{:S(2)}) async-start(bf16[16,128,256]{1,2,0:T(8,128)(2,1)} %copy.105), calls=%async_computation.6 | async-start | bytes 2097152 | tf_op jit(solution)/shard_map/all_to_all | solution.py:153
where the time goes:
time: 417 us; the launch traced here: 415 us
  blocking collectives  132 us (32%)
  waiting for transfers between devices  112 us (27%)
  matrix products  61.2 us (15%)
  local copies, waits for them, and re-layouts  46.1 us (11%)
  starting transfers between devices  39.2 us (9%)
  other arithmetic  22.4 us (5%)
    psum x1, blocking collectives, body(): total_terms = lax.psum(local_terms, ('step', 'ctx'))  82.3 us
    all_gather x1, blocking collectives, body(): full_sizes = lax.all_gather(merge_sizes, 'ctx', axis=0, tiled=True)  49.8 us
    all_to_all x1, waiting for transfers between devices, body(): lax.all_to_all(sent[0], 'ctx', split_axis=1, concat_axis=0, tiled=True)  25.9 us
    all_to_all x1, waiting for transfers between devices, body(): lax.all_to_all(sent[2], 'ctx', split_axis=1, concat_axis=0, tiled=True)  25.3 us
    all_to_all x1, waiting for transfers between devices, body(): lax.all_to_all(sent[1], 'ctx', split_axis=1, concat_axis=0, tiled=True)  23.7 us
    all_to_all x1, waiting for transfers between devices, body(): lax.all_to_all(homeward(dk_acc).astype(jnp.bfloat16), 'ctx', split_axis=0...  19.8 us
    all_to_all x1, waiting for transfers between devices, body(): lax.all_to_all(homeward(dq_acc).astype(jnp.bfloat16), 'ctx', split_axis=0...  17.8 us
    dot_general x5, matrix products, block_grads(): lax.dot_general(g_block, v_head, (((1,), (1,)), ((), ())), preferred_elem...  16.9 us
  transfers between devices with their start and end apart: 7, of which 5 were waited for; matrix products, arithmetic and copies ran while one was open for 8% of the time, Pallas kernels for 0%

commit v1 on v0

v1 whole, which is shorter than its diff:
```python
import functools
import math

import jax
import jax.numpy as jnp
from jax import lax
from jax.experimental import pallas as pl
from jax.experimental.pallas import tpu as pltpu
from jax.sharding import PartitionSpec as P

MESH = pl.DeviceIdType.MESH
DH = 128
NDEV = 16
ROWS = 128
TOK = NDEV * ROWS
HEADS = 20
BQ = 512
CK = 256
UNITS = TOK // BQ
SCALE = DH ** -0.5
NT = (((1,), (1,)), ((), ()))


def owner_of(h, core):
    early = h < 8
    last = h >= 16
    i = jnp.where(early, h, h - 8)
    z = 2 * (i // 2) + jnp.where(early, core, 1 - core)
    x = i % 2
    j = h - 16
    z = jnp.where(last, 2 * j + core, z)
    x = jnp.where(last, j % 2, x)
    return z * 2 + x


def kernel(
    coef_ref, q_ref, k_ref, v_ref, g_ref, ms_ref,
    dq_out, dk_out, dv_out, r_out,
    qb, kb, vb, gb, msb, kx, kt, s_buf, o_buf, ds_buf, dk_acc, dv_acc,
    dqs, dks, dvs, rmine, rother, rb,
    in_send, in_recv, ms_send, ms_recv, out_send, out_recv,
    rp_send, rp_recv, rb_send, rb_recv,
):
    me = lax.axis_index("ctx")
    step = lax.axis_index("step")
    core = lax.axis_index("grp") % 2
    z = me // 2
    x = me % 2
    early = (z + core) % 2 == 0
    double = jnp.logical_and(early, (z // 2) % 2 == x)
    first_head = jnp.where(early, 0, 8) + (z // 2) * 2 + x
    second_head = 16 + z // 2
    n_slots = jnp.where(double, 2, 1)

    barrier = pltpu.get_barrier_semaphore()

    def greet(j, _):
        pl.semaphore_signal(
            barrier, inc=1, device_id={"ctx": (me + j) % NDEV}, device_id_type=MESH
        )
        return 0

    lax.fori_loop(1, NDEV, greet, 0)
    pl.semaphore_signal(barrier, inc=1, device_id={"step": 1 - step}, device_id_type=MESH)
    pl.semaphore_wait(barrier, NDEV)

    my_rows = pl.ds(pl.multiple_of(me * ROWS, ROWS), ROWS)

    def ms_copy(j):
        return pltpu.make_async_remote_copy(
            src_ref=ms_ref, dst_ref=msb.at[me], send_sem=ms_send, recv_sem=ms_recv,
            device_id={"ctx": (me + j) % NDEV}, device_id_type=MESH,
        )

    def send_ms(j, _):
        ms_copy(j).start()
        return 0

    lax.fori_loop(1, NDEV, send_ms, 0)
    pltpu.make_async_copy(ms_ref, msb.at[me], ms_recv).start()

    def send_head(h):
        owner = owner_of(h, core)
        slot = h // 16
        cols = pl.ds(pl.multiple_of(h * DH, DH), DH)
        pairs = (
            (k_ref.at[0, :, cols], kb.at[slot, my_rows], 0),
            (v_ref.at[0, :, cols], vb.at[slot, my_rows], 1),
            (q_ref.at[0, :, cols], qb.at[slot, my_rows], 2),
            (g_ref.at[:, cols], gb.at[slot, my_rows], 3),
        )

        @pl.when(owner == me)
        def _():
            for src, dst, a in pairs:
                pltpu.make_async_copy(src, dst, in_recv.at[slot, a]).start()

        @pl.when(owner != me)
        def _():
            for src, dst, a in pairs:
                pltpu.make_async_remote_copy(
                    src_ref=src, dst_ref=dst, send_sem=in_send.at[h],
                    recv_sem=in_recv.at[slot, a],
                    device_id={"ctx": owner}, device_id_type=MESH,
                ).start()

    def send_early(j, _):
        send_head((me // 2 + j) % 8)
        return 0

    def send_late(j, _):
        send_head(8 + (me + j) % 12)
        return 0

    lax.fori_loop(0, 8, send_early, 0)
    lax.fori_loop(0, 12, send_late, 0)

    pltpu.make_async_copy(msb, msb, ms_recv).wait()
    lane = lax.broadcasted_iota(jnp.int32, (ROWS, ROWS), 1)
    row = lax.broadcasted_iota(jnp.int32, (ROWS, ROWS), 0)

    def extend(t, _):
        logs = jnp.log(msb[t].astype(jnp.float32)) * (1.0 / SCALE)
        spread = jnp.where(lane == row, jnp.broadcast_to(logs, (ROWS, ROWS)), 0.0)
        column = jnp.sum(spread, axis=1, keepdims=True)
        hi = column.astype(jnp.bfloat16).astype(jnp.float32)
        rest = column - hi
        mid = rest.astype(jnp.bfloat16).astype(jnp.float32)
        low = rest - mid
        ext = jnp.where(lane == 0, hi, jnp.where(lane == 1, mid, jnp.where(lane == 2, low, 0.0)))
        kx[pl.ds(pl.multiple_of(t * ROWS, ROWS), ROWS), :] = ext.astype(jnp.bfloat16)
        return 0

    lax.fori_loop(0, NDEV, extend, 0)

    ones = jnp.ones((BQ, DH), jnp.bfloat16)

    def do_slot(slot, _):
        h = jnp.where(slot == 0, first_head, second_head)
        coef = coef_ref[h]
        cols = pl.ds(pl.multiple_of(h * DH, DH), DH)
        for a, buf in enumerate((kb, vb, qb, gb)):
            pltpu.make_async_copy(buf.at[slot], buf.at[slot], in_recv.at[slot, a]).wait()

        def transpose_keys(t, _):
            rows = pl.ds(pl.multiple_of(t * ROWS, ROWS), ROWS)
            kt[:, rows] = kb[slot, rows, :].astype(jnp.float32).T.astype(jnp.bfloat16)
            dk_acc[rows, :] = jnp.zeros((ROWS, DH), jnp.float32)
            dv_acc[rows, :] = jnp.zeros((ROWS, DH), jnp.float32)
            return 0

        lax.fori_loop(0, NDEV, transpose_keys, 0)

        def send_rows(src_buf, dst_out, a, t):
            rows = pl.ds(pl.multiple_of(t * ROWS, ROWS), ROWS)
            src = src_buf.at[slot, rows]
            dst = dst_out.at[0, :, cols]

            @pl.when(t == me)
            def _():
                pltpu.make_async_copy(src, dst, out_recv.at[a]).start()

            @pl.when(t != me)
            def _():
                pltpu.make_async_remote_copy(
                    src_ref=src, dst_ref=dst, send_sem=out_send.at[slot, a],
                    recv_sem=out_recv.at[a], device_id={"ctx": t}, device_id_type=MESH,
                ).start()

        def unit(b, r_sum):
            q_rows = pl.ds(pl.multiple_of(b * BQ, BQ), BQ)
            q_ext = jnp.concatenate([qb[slot, q_rows, :], ones], axis=1)

            def pass1(c, top):
                rows = pl.ds(pl.multiple_of(c * CK, CK), CK)
                k_ext = jnp.concatenate([kb[slot, rows, :], kx[rows, :]], axis=1)
                s = lax.dot_general(k_ext, q_ext, NT, preferred_element_type=jnp.float32)
                s_buf[rows, :] = s
                return jnp.maximum(top, jnp.max(s.reshape(CK // 8, 8, BQ), axis=0))

            top = lax.fori_loop(
                0, TOK // CK, pass1, jnp.full((8, BQ), -jnp.inf, jnp.float32)
            )
            top = jnp.max(top, axis=0, keepdims=True)

            def pass2(c, carry):
                l_sum, rd_sum = carry
                rows = pl.ds(pl.multiple_of(c * CK, CK), CK)
                o = lax.dot_general(
                    vb[slot, rows, :], gb[slot, q_rows, :], NT,
                    preferred_element_type=jnp.float32,
                )
                e = jnp.exp2((s_buf[rows, :] - top) * (SCALE * math.log2(math.e)))
                s_buf[rows, :] = e
                o_buf[rows, :] = o
                l_sum = l_sum + jnp.sum(e.reshape(CK // 8, 8, BQ), axis=0)
                rd_sum = rd_sum + jnp.sum((e * o).reshape(CK // 8, 8, BQ), axis=0)
                return (l_sum, rd_sum)

            zero = jnp.zeros((8, BQ), jnp.float32)
            l_sum, rd_sum = lax.fori_loop(0, TOK // CK, pass2, (zero, zero))
            inv = 1.0 / jnp.sum(l_sum, axis=0, keepdims=True)
            rd = jnp.sum(rd_sum, axis=0, keepdims=True) * inv
            for i in range(BQ // DH):
                r_sum = r_sum + rd[:, i * DH:(i + 1) * DH]
            inv_col = jnp.concatenate(
                [
                    jnp.broadcast_to(inv[:, i * DH:(i + 1) * DH], (DH, DH)).T
                    for i in range(BQ // DH)
                ],
                axis=0,
            ) * coef
            g_scaled = (gb[slot, q_rows, :].astype(jnp.float32) * inv_col).astype(jnp.bfloat16)
            inv_col = inv_col * SCALE
            q_scaled = (qb[slot, q_rows, :].astype(jnp.float32) * inv_col).astype(jnp.bfloat16)

            def pass3(c, _):
                rows = pl.ds(pl.multiple_of(c * CK, CK), CK)
                e = s_buf[rows, :]
                ds = (e * (o_buf[rows, :] - rd)).astype(jnp.bfloat16)
                ds_buf[rows, :] = ds
                dv_acc[rows, :] += jnp.dot(
                    e.astype(jnp.bfloat16), g_scaled, preferred_element_type=jnp.float32
                )
                dk_acc[rows, :] += jnp.dot(ds, q_scaled, preferred_element_type=jnp.float32)
                return 0

            lax.fori_loop(0, TOK // CK, pass3, 0)
            dqt = jnp.dot(kt[...], ds_buf[...], preferred_element_type=jnp.float32)
            dqs[slot, q_rows, :] = (dqt.T * inv_col).astype(jnp.bfloat16)
            for i in range(BQ // ROWS):
                send_rows(dqs, dq_out, 0, b * (BQ // ROWS) + i)
            return r_sum

        r_sum = lax.fori_loop(0, UNITS, unit, jnp.zeros((1, DH), jnp.float32))

        def finish(t, _):
            rows = pl.ds(pl.multiple_of(t * ROWS, ROWS), ROWS)
            dks[slot, rows, :] = dk_acc[rows, :].astype(jnp.bfloat16)
            dvs[slot, rows, :] = dv_acc[rows, :].astype(jnp.bfloat16)
            send_rows(dks, dk_out, 1, t)
            send_rows(dvs, dv_out, 2, t)
            return 0

        lax.fori_loop(0, NDEV, finish, 0)
        rmine[slot] = jnp.broadcast_to(jnp.sum(r_sum, axis=1, keepdims=True), (8, DH))
        partner_copy(slot).start()
        return 0

    def partner_copy(slot):
        return pltpu.make_async_remote_copy(
            src_ref=rmine.at[slot], dst_ref=rother.at[slot],
            send_sem=rp_send.at[slot], recv_sem=rp_recv.at[slot],
            device_id={"step": 1 - step}, device_id_type=MESH,
        )

    lax.fori_loop(0, n_slots, do_slot, 0)

    sign = jnp.where(step == 1, 1.0, -1.0).astype(jnp.float32)

    def spread_router(slot, _):
        h = jnp.where(slot == 0, first_head, second_head)
        partner_copy(slot).wait()
        rmine[slot] = (rmine[slot] - rother[slot]) * sign

        def send(j, _):
            pltpu.make_async_remote_copy(
                src_ref=rmine.at[slot], dst_ref=rb.at[h],
                send_sem=rb_send.at[slot], recv_sem=rb_recv,
                device_id={"ctx": (me + j) % NDEV}, device_id_type=MESH,
            ).start()
            return 0

        lax.fori_loop(1, NDEV, send, 0)
        pltpu.make_async_copy(rmine.at[slot], rb.at[h], rb_recv).start()
        return 0

    lax.fori_loop(0, n_slots, spread_router, 0)

    pltpu.make_async_copy(msb.at[pl.ds(0, NDEV - 1)], msb.at[pl.ds(0, NDEV - 1)], ms_send).wait()

    def sent_head(h, _):
        @pl.when(owner_of(h, core) != me)
        def _():
            pltpu.make_async_copy(
                kb.at[0, pl.ds(0, 4 * ROWS)], kb.at[0, pl.ds(0, 4 * ROWS)], in_send.at[h]
            ).wait()

        return 0

    lax.fori_loop(0, HEADS, sent_head, 0)

    def sent_slot(slot, _):
        for a, buf in enumerate((dqs, dks, dvs)):
            part = buf.at[slot, pl.ds(0, TOK - ROWS)]
            pltpu.make_async_copy(part, part, out_send.at[slot, a]).wait()
        part = rb.at[pl.ds(0, NDEV - 1)]
        pltpu.make_async_copy(part, part, rb_send.at[slot]).wait()
        return 0

    lax.fori_loop(0, n_slots, sent_slot, 0)

    pltpu.make_async_copy(rb, rb, rb_recv).wait()
    r_out[...] = rb[...]
    for a, out in enumerate((dq_out, dk_out, dv_out)):
        pltpu.make_async_copy(out, out, out_recv.at[a]).wait()


def body(queries, keys, values, cotangent, merge_sizes, router_logits, gate_plan):
    step = lax.axis_index("step")
    beta = jnp.where(gate_plan == 1, jax.nn.sigmoid(router_logits), jnp.float32(1.0))
    coef = jnp.where(step == 1, beta, 1.0 - beta)
    shape = queries.shape
    bf16, f32 = jnp.bfloat16, jnp.float32
    anywhere = pl.BlockSpec(memory_space=pl.ANY)
    dma = pltpu.SemaphoreType.DMA
    dq, dk, dv, r = pl.pallas_call(
        kernel,
        out_shape=[
            jax.ShapeDtypeStruct(shape, bf16),
            jax.ShapeDtypeStruct(shape, bf16),
            jax.ShapeDtypeStruct(shape, bf16),
            jax.ShapeDtypeStruct((HEADS, 8, DH), f32),
        ],
        in_specs=[pl.BlockSpec(memory_space=pltpu.SMEM)] + [anywhere] * 5,
        out_specs=[anywhere] * 3 + [pl.BlockSpec(memory_space=pltpu.VMEM)],
        scratch_shapes=[
            pltpu.VMEM((2, TOK, DH), bf16),
            pltpu.VMEM((2, TOK, DH), bf16),
            pltpu.VMEM((2, TOK, DH), bf16),
            pltpu.VMEM((2, TOK, DH), bf16),
            pltpu.VMEM((NDEV, 1, ROWS), jnp.int32),
            pltpu.VMEM((TOK, DH), bf16),
            pltpu.VMEM((DH, TOK), bf16),
            pltpu.VMEM((TOK, BQ), f32),
            pltpu.VMEM((TOK, BQ), f32),
            pltpu.VMEM((TOK, BQ), bf16),
            pltpu.VMEM((TOK, DH), f32),
            pltpu.VMEM((TOK, DH), f32),
            pltpu.VMEM((2, TOK, DH), bf16),
            pltpu.VMEM((2, TOK, DH), bf16),
            pltpu.VMEM((2, TOK, DH), bf16),
            pltpu.VMEM((2, 8, DH), f32),
            pltpu.VMEM((2, 8, DH), f32),
            pltpu.VMEM((HEADS, 8, DH), f32),
            dma((HEADS,)),
            dma((2, 4)),
            dma, dma,
            dma((2, 3)),
            dma((3,)),
            dma((2,)), dma((2,)),
            dma((2,)), dma,
        ],
        compiler_params=pltpu.CompilerParams(
            collective_id=0, has_side_effects=True, vmem_limit_bytes=48 * 1024 * 1024
        ),
        cost_estimate=pl.CostEstimate(
            flops=7_000_000_000, bytes_accessed=5_000_000, transcendentals=5_000_000
        ),
    )(coef, queries, keys, values, cotangent, merge_sizes.reshape(1, ROWS))
    router_grad = beta * (1.0 - beta) * r[:, 0, 0] / math.sqrt(TOK)
    return (dq, dk, dv, router_grad)


def solution(mesh):
    return jax.shard_map(
        body,
        mesh=mesh,
        in_specs=(
            P("step", ("grp", "ctx"), None),
            P("step", ("grp", "ctx"), None),
            P("step", ("grp", "ctx"), None),
            P(("grp", "ctx"), None),
            P(("grp", "ctx")),
            P(),
            P(),
        ),
        out_specs=(
            P("step", ("grp", "ctx"), None),
            P("step", ("grp", "ctx"), None),
            P("step", ("grp", "ctx"), None),
            P("grp"),
        ),
        check_vma=False,
    )
```

time: 417 us -> 144 us (0.35)
  Pallas kernels: 0 us -> 134 us
  blocking collectives: 132 us -> 0 us
  waiting for transfers between devices: 112 us -> 0 us
  matrix products: 61.2 us -> 0 us
  starting transfers between devices: 39.2 us -> 0 us
  local copies, waits for them, and re-layouts: 46.1 us -> 8.4 us
  other arithmetic: 22.4 us -> 0.53 us
    pallas_call x0 -> x1, Pallas kernels: none -> 134 us  [body(): pl.pallas_call(kernel, out_shape=[jax.ShapeDtypeStruct(shape, bf16), jax....]
    all_to_all x7 -> x0, waiting for transfers between devices: 112 us -> none  [the longest x1 25.9 us: body(): lax.all_to_all(sent[0], 'ctx', split_axis=1, concat_axis=0, tiled=True)]
    psum x1 -> x0, blocking collectives: 82.3 us -> none  [body(): total_terms = lax.psum(local_terms, ('step', 'ctx'))]
    dot_general x29 -> x0, matrix products: 61.2 us -> none  [the longest x5 16.9 us: block_grads(): lax.dot_general(g_block, v_head, (((1,), (1,)), ((), ())), preferred_elem...]
    all_gather x1 -> x0, blocking collectives: 49.8 us -> none  [body(): full_sizes = lax.all_gather(merge_sizes, 'ctx', axis=0, tiled=True)]
    all_to_all x7 -> x0, starting transfers between devices: 39.2 us -> none  [the longest x1 11.3 us: body(): lax.all_to_all(sent[0], 'ctx', split_axis=1, concat_axis=0, tiled=True)]
    convert_element_type x7 -> x0, other arithmetic: 12.1 us -> none  [the longest x5 11.8 us: block_grads(): dscore = (coef * probs * (outer - rowdot[:, None])).astype(jnp.bfloat16)]
    reshape x8 -> x0, local copies, waits for them, and re-layouts: 9.49 us -> none  [the longest x3 4.84 us: assemble(): piece.astype(jnp.float32).reshape(devices, tok_rows, slot_count, head_size)]
  transfers between devices with their start and end apart: 7 -> 0, of which waited for: 5 -> 0; matrix products, arithmetic and copies ran while one was open for 8% -> 0% of each run, Pallas kernels for 0% -> 0%
where the time goes in v1:
time: 144 us
  Pallas kernels  134 us (93%)
  local copies, waits for them, and re-layouts  8.4 us (6%)
    pallas_call x1, Pallas kernels, body(): pl.pallas_call(kernel, out_shape=[jax.ShapeDtypeStruct(shape, bf16), jax....  134 us
    unnamed x17, local copies, waits for them, and re-layouts  8.17 us

profile of v1, /device:TPU:56, one launch (start us, length us, event | category | flops | bytes accessed | tf_op | source)
XLA Modules:
  0.0 144.0 jit_solution(11030783166193101660)
XLA Ops:
  0.6 0.0 copy-start.5
  0.6 0.0 copy-start.6
  0.7 0.6 copy-done.5
  1.3 0.0 copy-done.6
  1.3 0.0 copy-start.4
  1.3 0.7 copy-done.4
  2.0 0.0 copy-start
  2.0 1.1 copy-done
  3.1 0.0 copy-start.1
  3.1 1.1 copy-done.1
  4.2 0.0 copy-start.2
  4.2 1.1 copy-done.2
  5.2 0.0 copy-start.3
  5.2 1.1 copy-done.3
  6.3 134.4 %shard_map.102 = (bf16[1,128,2560]{2,1,0:T(8,128)(2,1)S(1)}, bf16[1,128,2560]{2,1,0:T(8,128)(2,1)S(1)}, bf16[1,128,2560]{2,1,0:T(8,128)(2,1)S(1)}, f32[20,8,128]{2,1,0:T(8,128)S(1)}) custom-call(f32[20]{0:T(128)S(1)} %get-tuple-element.12.coef_ref, bf16[1,128,2560]{2,1,0:T(8,128)(2,1)S(1)} %copy-done, bf16[1,128,2560]{2,1,0:T(8,128)(2,1)S(1)} %copy-done.1, ...), custom_call_target="tpu_custom_call" | custom-call | flops 7000000000 | bytes 5000000 | tf_op jit(solution)/shard_map/pallas_call | solution.py:317
  140.7 0.2 slice_reduce_fusion
  140.9 0.5 fusion.1
  141.5 0.8 copy.14
  142.3 0.8 copy.15
  143.1 0.8 copy.16
  (1 shorter events, 0.0 us)
Async XLA Ops:
  0.6 0.7 copy-start.5
  0.6 0.7 copy-start.6
  1.3 0.7 copy-start.4
  2.0 1.1 copy-start
  3.1 1.1 copy-start.1
  4.2 1.1 copy-start.2
  5.2 1.1 copy-start.3

commit v2 on v1

--- a/solution.py
+++ b/solution.py
@@ -15,7 +15,8 @@
 TOK = NDEV * ROWS
 HEADS = 20
 BQ = 512
-CK = 256
+CK = 1024
+HALF = ROWS // 2
 UNITS = TOK // BQ
 SCALE = DH ** -0.5
 NT = (((1,), (1,)), ((), ()))
@@ -29,16 +30,16 @@
     x = i % 2
     j = h - 16
     z = jnp.where(last, 2 * j + core, z)
-    x = jnp.where(last, j % 2, x)
+    x = jnp.where(last, core, x)
     return z * 2 + x
 
 
 def kernel(
-    coef_ref, q_ref, k_ref, v_ref, g_ref, ms_ref,
+    logit_ref, gate_ref, q_ref, k_ref, v_ref, g_ref, ms_ref,
     dq_out, dk_out, dv_out, r_out,
     qb, kb, vb, gb, msb, kx, kt, s_buf, o_buf, ds_buf, dk_acc, dv_acc,
-    dqs, dks, dvs, rmine, rother, rb,
-    in_send, in_recv, ms_send, ms_recv, out_send, out_recv,
+    dqs, dks, dvs, rmine, rb, rrow, rother,
+    in_send, in_recv, gf_send, gf_recv, ms_send, ms_recv, out_send, out_recv,
     rp_send, rp_recv, rb_send, rb_recv,
 ):
     me = lax.axis_index("ctx")
@@ -47,7 +48,7 @@
     z = me // 2
     x = me % 2
     early = (z + core) % 2 == 0
-    double = jnp.logical_and(early, (z // 2) % 2 == x)
+    double = jnp.logical_and(early, x == core)
     first_head = jnp.where(early, 0, 8) + (z // 2) * 2 + x
     second_head = 16 + z // 2
     n_slots = jnp.where(double, 2, 1)
@@ -79,41 +80,59 @@
     lax.fori_loop(1, NDEV, send_ms, 0)
     pltpu.make_async_copy(ms_ref, msb.at[me], ms_recv).start()
 
-    def send_head(h):
+    def send_pairs(h, pairs):
         owner = owner_of(h, core)
-        slot = h // 16
-        cols = pl.ds(pl.multiple_of(h * DH, DH), DH)
-        pairs = (
-            (k_ref.at[0, :, cols], kb.at[slot, my_rows], 0),
-            (v_ref.at[0, :, cols], vb.at[slot, my_rows], 1),
-            (q_ref.at[0, :, cols], qb.at[slot, my_rows], 2),
-            (g_ref.at[:, cols], gb.at[slot, my_rows], 3),
-        )
 
         @pl.when(owner == me)
         def _():
-            for src, dst, a in pairs:
-                pltpu.make_async_copy(src, dst, in_recv.at[slot, a]).start()
+            for src, dst, sem in pairs:
+                pltpu.make_async_copy(src, dst, sem).start()
 
         @pl.when(owner != me)
         def _():
-            for src, dst, a in pairs:
+            for src, dst, sem in pairs:
                 pltpu.make_async_remote_copy(
-                    src_ref=src, dst_ref=dst, send_sem=in_send.at[h],
-                    recv_sem=in_recv.at[slot, a],
+                    src_ref=src, dst_ref=dst, send_sem=in_send.at[h], recv_sem=sem,
                     device_id={"ctx": owner}, device_id_type=MESH,
                 ).start()
 
-    def send_early(j, _):
-        send_head((me // 2 + j) % 8)
-        return 0
-
-    def send_late(j, _):
-        send_head(8 + (me + j) % 12)
-        return 0
-
-    lax.fori_loop(0, 8, send_early, 0)
-    lax.fori_loop(0, 12, send_late, 0)
+    def columns(h):
+        return pl.ds(pl.multiple_of(h * DH, DH), DH)
+
+    def send_g(h):
+        slot = h // 16
+        rows = pl.ds(pl.multiple_of(step * HALF, HALF), HALF)
+        send_pairs(h, ((g_ref.at[rows, columns(h)], gb.at[slot, me, step], in_recv.at[slot, 3]),))
+
+    def send_qkv(h):
+        slot = h // 16
+        cols = columns(h)
+        send_pairs(h, (
+            (k_ref.at[0, :, cols], kb.at[slot, my_rows], in_recv.at[slot, 0]),
+            (v_ref.at[0, :, cols], vb.at[slot, my_rows], in_recv.at[slot, 1]),
+            (q_ref.at[0, :, cols], qb.at[slot, my_rows], in_recv.at[slot, 2]),
+        ))
+
+    def loop(send, first, count, start):
+        def one(j, _):
+            send(first + (start + j) % count)
+            return 0
+
+        lax.fori_loop(0, count, one, 0)
+
+    loop(send_g, 0, 8, z)
+    loop(send_g, 16, 4, z // 2)
+    loop(send_qkv, 0, 8, z)
+    loop(send_g, 8, 8, z)
+    loop(send_qkv, 16, 4, z // 2)
+    loop(send_qkv, 8, 8, z)
+
+    def forward_g(slot):
+        return pltpu.make_async_remote_copy(
+            src_ref=gb.at[slot, :, step], dst_ref=gb.at[slot, :, step],
+            send_sem=gf_send.at[slot], recv_sem=gf_recv.at[slot],
+            device_id={"step": 1 - step}, device_id_type=MESH,
+        )
 
     pltpu.make_async_copy(msb, msb, ms_recv).wait()
     lane = lax.broadcasted_iota(jnp.int32, (ROWS, ROWS), 1)
@@ -133,14 +152,26 @@
 
     lax.fori_loop(0, NDEV, extend, 0)
 
+    def pass_g_on(slot, _):
+        half = gb.at[slot, :, step]
+        pltpu.make_async_copy(half, half, in_recv.at[slot, 3]).wait()
+        forward_g(slot).start()
+        return 0
+
+    lax.fori_loop(0, n_slots, pass_g_on, 0)
+
+    beta = jnp.where(gate_ref[...] == 1, jax.nn.sigmoid(logit_ref[...]), 1.0)
+    coef_row = jnp.where(step == 1, beta, 1.0 - beta)
+    head_lane = lax.broadcasted_iota(jnp.int32, (1, HEADS), 1)
     ones = jnp.ones((BQ, DH), jnp.bfloat16)
 
     def do_slot(slot, _):
         h = jnp.where(slot == 0, first_head, second_head)
-        coef = coef_ref[h]
-        cols = pl.ds(pl.multiple_of(h * DH, DH), DH)
-        for a, buf in enumerate((kb, vb, qb, gb)):
+        coef = jnp.sum(jnp.where(head_lane == h, coef_row, 0.0), axis=1, keepdims=True)
+        cols = columns(h)
+        for a, buf in enumerate((kb, vb, qb)):
             pltpu.make_async_copy(buf.at[slot], buf.at[slot], in_recv.at[slot, a]).wait()
+        forward_g(slot).wait_recv()
 
         def transpose_keys(t, _):
             rows = pl.ds(pl.multiple_of(t * ROWS, ROWS), ROWS)
@@ -169,6 +200,7 @@
 
         def unit(b, r_sum):
             q_rows = pl.ds(pl.multiple_of(b * BQ, BQ), BQ)
+            g_blk = gb[slot, pl.ds(b * (BQ // ROWS), BQ // ROWS)].reshape(BQ, DH)
             q_ext = jnp.concatenate([qb[slot, q_rows, :], ones], axis=1)
 
             def pass1(c, top):
@@ -187,7 +219,7 @@
                 l_sum, rd_sum = carry
                 rows = pl.ds(pl.multiple_of(c * CK, CK), CK)
                 o = lax.dot_general(
-                    vb[slot, rows, :], gb[slot, q_rows, :], NT,
+                    vb[slot, rows, :], g_blk, NT,
                     preferred_element_type=jnp.float32,
                 )
                 e = jnp.exp2((s_buf[rows, :] - top) * (SCALE * math.log2(math.e)))
@@ -203,14 +235,31 @@
             rd = jnp.sum(rd_sum, axis=0, keepdims=True) * inv
             for i in range(BQ // DH):
                 r_sum = r_sum + rd[:, i * DH:(i + 1) * DH]
+
+            @pl.when(b == UNITS - 1)
+            def _():
+                rmine[slot] = r_sum
+
+                def send_r(j, _):
+                    pltpu.make_async_remote_copy(
+                        src_ref=rmine.at[slot], dst_ref=rb.at[h],
+                        send_sem=rb_send.at[slot], recv_sem=rb_recv,
+                        device_id={"ctx": (me + j) % NDEV}, device_id_type=MESH,
+                    ).start()
+                    return 0
+
+                lax.fori_loop(1, NDEV, send_r, 0)
+                pltpu.make_async_copy(rmine.at[slot], rb.at[h], rb_recv).start()
+
+            inv = inv * coef
             inv_col = jnp.concatenate(
                 [
                     jnp.broadcast_to(inv[:, i * DH:(i + 1) * DH], (DH, DH)).T
                     for i in range(BQ // DH)
                 ],
                 axis=0,
-            ) * coef
-            g_scaled = (gb[slot, q_rows, :].astype(jnp.float32) * inv_col).astype(jnp.bfloat16)
+            )
+            g_scaled = (g_blk.astype(jnp.float32) * inv_col).astype(jnp.bfloat16)
             inv_col = inv_col * SCALE
             q_scaled = (qb[slot, q_rows, :].astype(jnp.float32) * inv_col).astype(jnp.bfloat16)
 
@@ -225,65 +274,61 @@
                 dk_acc[rows, :] += jnp.dot(ds, q_scaled, preferred_element_type=jnp.float32)
                 return 0
 
-            lax.fori_loop(0, TOK // CK, pass3, 0)
+            def finish(t, _):
+                rows = pl.ds(pl.multiple_of(t * ROWS, ROWS), ROWS)
+                dks[slot, rows, :] = dk_acc[rows, :].astype(jnp.bfloat16)
+                dvs[slot, rows, :] = dv_acc[rows, :].astype(jnp.bfloat16)
+                send_rows(dks, dk_out, 1, t)
+                send_rows(dvs, dv_out, 2, t)
+                return 0
+
+            def pass3_send(c, _):
+                pass3(c, 0)
+
+                @pl.when(b == UNITS - 1)
+                def _():
+                    lax.fori_loop(c * (CK // ROWS), (c + 1) * (CK // ROWS), finish, 0)
+
+                return 0
+
+            lax.fori_loop(0, TOK // CK, pass3_send, 0)
             dqt = jnp.dot(kt[...], ds_buf[...], preferred_element_type=jnp.float32)
             dqs[slot, q_rows, :] = (dqt.T * inv_col).astype(jnp.bfloat16)
-            for i in range(BQ // ROWS):
+
+            def send_dq(i, _):
                 send_rows(dqs, dq_out, 0, b * (BQ // ROWS) + i)
+                return 0
+
+            lax.fori_loop(0, BQ // ROWS, send_dq, 0)
             return r_sum
 
-        r_sum = lax.fori_loop(0, UNITS, unit, jnp.zeros((1, DH), jnp.float32))
-
-        def finish(t, _):
-            rows = pl.ds(pl.multiple_of(t * ROWS, ROWS), ROWS)
-            dks[slot, rows, :] = dk_acc[rows, :].astype(jnp.bfloat16)
-            dvs[slot, rows, :] = dv_acc[rows, :].astype(jnp.bfloat16)
-            send_rows(dks, dk_out, 1, t)
-            send_rows(dvs, dv_out, 2, t)
-            return 0
-
-        lax.fori_loop(0, NDEV, finish, 0)
-        rmine[slot] = jnp.broadcast_to(jnp.sum(r_sum, axis=1, keepdims=True), (8, DH))
-        partner_copy(slot).start()
-        return 0
-
-    def partner_copy(slot):
-        return pltpu.make_async_remote_copy(
-            src_ref=rmine.at[slot], dst_ref=rother.at[slot],
-            send_sem=rp_send.at[slot], recv_sem=rp_recv.at[slot],
-            device_id={"step": 1 - step}, device_id_type=MESH,
-        )
+        lax.fori_loop(0, UNITS, unit, jnp.zeros((1, DH), jnp.float32))
+        return 0
 
     lax.fori_loop(0, n_slots, do_slot, 0)
 
-    sign = jnp.where(step == 1, 1.0, -1.0).astype(jnp.float32)
-
-    def spread_router(slot, _):
-        h = jnp.where(slot == 0, first_head, second_head)
-        partner_copy(slot).wait()
-        rmine[slot] = (rmine[slot] - rother[slot]) * sign
-
-        def send(j, _):
-            pltpu.make_async_remote_copy(
-                src_ref=rmine.at[slot], dst_ref=rb.at[h],
-                send_sem=rb_send.at[slot], recv_sem=rb_recv,
-                device_id={"ctx": (me + j) % NDEV}, device_id_type=MESH,
-            ).start()
-            return 0
-
-        lax.fori_loop(1, NDEV, send, 0)
-        pltpu.make_async_copy(rmine.at[slot], rb.at[h], rb_recv).start()
-        return 0
-
-    lax.fori_loop(0, n_slots, spread_router, 0)
+    pltpu.make_async_copy(rb, rb, rb_recv).wait()
+    sums = jnp.sum(rb[...], axis=2)
+    diagonal = (
+        lax.broadcasted_iota(jnp.int32, (HEADS, DH), 0)
+        == lax.broadcasted_iota(jnp.int32, (HEADS, DH), 1)
+    )
+    rrow[...] = jnp.sum(jnp.where(diagonal, sums, 0.0), axis=0, keepdims=True)
+    to_partner = pltpu.make_async_remote_copy(
+        src_ref=rrow, dst_ref=rother, send_sem=rp_send, recv_sem=rp_recv,
+        device_id={"step": 1 - step}, device_id_type=MESH,
+    )
+    to_partner.start()
 
     pltpu.make_async_copy(msb.at[pl.ds(0, NDEV - 1)], msb.at[pl.ds(0, NDEV - 1)], ms_send).wait()
+
+    sent = kb.at[0, pl.ds(0, 3 * ROWS + HALF)]
 
     def sent_head(h, _):
         @pl.when(owner_of(h, core) != me)
         def _():
             pltpu.make_async_copy(
-                kb.at[0, pl.ds(0, 4 * ROWS)], kb.at[0, pl.ds(0, 4 * ROWS)], in_send.at[h]
+                sent, sent, in_send.at[h]
             ).wait()
 
         return 0
@@ -296,23 +341,44 @@
             pltpu.make_async_copy(part, part, out_send.at[slot, a]).wait()
         part = rb.at[pl.ds(0, NDEV - 1)]
         pltpu.make_async_copy(part, part, rb_send.at[slot]).wait()
+        forward_g(slot).wait_send()
         return 0
 
     lax.fori_loop(0, n_slots, sent_slot, 0)
 
-    pltpu.make_async_copy(rb, rb, rb_recv).wait()
-    r_out[...] = rb[...]
+    to_partner.wait()
+    sign = jnp.where(step == 1, 1.0, -1.0).astype(jnp.float32)
+    total = (rrow[...] - rother[...]) * sign
+    r_out[...] = beta * (1.0 - beta) * total[:, :HEADS] * (1.0 / math.sqrt(TOK))
     for a, out in enumerate((dq_out, dk_out, dv_out)):
         pltpu.make_async_copy(out, out, out_recv.at[a]).wait()
 
 
+def hand_over(
+    dq_in, dk_in, dv_in, r_in, dq_out, dk_out, dv_out, r_out, held, r_held, sems_in, sems_out,
+):
+    into, onward = [pltpu.make_async_copy(r_in, r_held, sems_in.at[0])], []
+    onward.append(pltpu.make_async_copy(r_held, r_out, sems_out.at[0]))
+    for a, (src, dst) in enumerate(((dq_in, dq_out), (dk_in, dk_out), (dv_in, dv_out))):
+        for i in range(2):
+            rows = pl.ds(i * HALF, HALF)
+            n = 1 + 2 * a + i
+            into.append(pltpu.make_async_copy(src.at[0, rows], held.at[a, rows], sems_in.at[n]))
+            onward.append(pltpu.make_async_copy(held.at[a, rows], dst.at[0, rows], sems_out.at[n]))
+    for copy in into:
+        copy.start()
+    for copy, after in zip(into, onward):
+        copy.wait()
+        after.start()
+    for copy in onward:
+        copy.wait()
+
+
 def body(queries, keys, values, cotangent, merge_sizes, router_logits, gate_plan):
-    step = lax.axis_index("step")
-    beta = jnp.where(gate_plan == 1, jax.nn.sigmoid(router_logits), jnp.float32(1.0))
-    coef = jnp.where(step == 1, beta, 1.0 - beta)
     shape = queries.shape
     bf16, f32 = jnp.bfloat16, jnp.float32
     anywhere = pl.BlockSpec(memory_space=pl.ANY)
+    whole = pl.BlockSpec(memory_space=pltpu.VMEM)
     dma = pltpu.SemaphoreType.DMA
     dq, dk, dv, r = pl.pallas_call(
         kernel,
@@ -320,15 +386,15 @@
             jax.ShapeDtypeStruct(shape, bf16),
             jax.ShapeDtypeStruct(shape, bf16),
             jax.ShapeDtypeStruct(shape, bf16),
-            jax.ShapeDtypeStruct((HEADS, 8, DH), f32),
+            jax.ShapeDtypeStruct((1, HEADS), f32),
         ],
-        in_specs=[pl.BlockSpec(memory_space=pltpu.SMEM)] + [anywhere] * 5,
-        out_specs=[anywhere] * 3 + [pl.BlockSpec(memory_space=pltpu.VMEM)],
+        in_specs=[whole, whole] + [anywhere] * 5,
+        out_specs=[anywhere] * 3 + [whole],
         scratch_shapes=[
             pltpu.VMEM((2, TOK, DH), bf16),
             pltpu.VMEM((2, TOK, DH), bf16),
             pltpu.VMEM((2, TOK, DH), bf16),
-            pltpu.VMEM((2, TOK, DH), bf16),
+            pltpu.VMEM((2, NDEV, 2, HALF, DH), bf16),
             pltpu.VMEM((NDEV, 1, ROWS), jnp.int32),
             pltpu.VMEM((TOK, DH), bf16),
             pltpu.VMEM((DH, TOK), bf16),
@@ -340,26 +406,41 @@
             pltpu.VMEM((2, TOK, DH), bf16),
             pltpu.VMEM((2, TOK, DH), bf16),
             pltpu.VMEM((2, TOK, DH), bf16),
-            pltpu.VMEM((2, 8, DH), f32),
-            pltpu.VMEM((2, 8, DH), f32),
-            pltpu.VMEM((HEADS, 8, DH), f32),
+            pltpu.VMEM((2, 1, DH), f32),
+            pltpu.VMEM((HEADS, 1, DH), f32),
+            pltpu.VMEM((1, DH), f32),
+            pltpu.VMEM((1, DH), f32),
             dma((HEADS,)),
             dma((2, 4)),
+            dma((2,)), dma((2,)),
             dma, dma,
             dma((2, 3)),
             dma((3,)),
-            dma((2,)), dma((2,)),
+            dma, dma,
             dma((2,)), dma,
         ],
         compiler_params=pltpu.CompilerParams(
-            collective_id=0, has_side_effects=True, vmem_limit_bytes=48 * 1024 * 1024
+            collective_id=0, has_side_effects=True, vmem_limit_bytes=60 * 1024 * 1024
         ),
         cost_estimate=pl.CostEstimate(
             flops=7_000_000_000, bytes_accessed=5_000_000, transcendentals=5_000_000
         ),
-    )(coef, queries, keys, values, cotangent, merge_sizes.reshape(1, ROWS))
-    router_grad = beta * (1.0 - beta) * r[:, 0, 0] / math.sqrt(TOK)
-    return (dq, dk, dv, router_grad)
+    )(
+        router_logits.reshape(1, HEADS), gate_plan.reshape(1, HEADS),
+        queries, keys, values, cotangent, merge_sizes.reshape(1, ROWS),
+    )
+    dq, dk, dv, r = pl.pallas_call(
+        hand_over,
+        out_shape=[jax.ShapeDtypeStruct(shape, bf16)] * 3
+        + [jax.ShapeDtypeStruct((1, HEADS), f32)],
+        in_specs=[anywhere] * 4,
+        out_specs=[anywhere] * 4,
+        scratch_shapes=[
+            pltpu.VMEM((3,) + shape[1:], bf16), pltpu.VMEM((1, HEADS), f32), dma((7,)), dma((7,)),
+        ],
+        compiler_params=pltpu.CompilerParams(vmem_limit_bytes=60 * 1024 * 1024),
+    )(dq, dk, dv, r)
+    return (dq, dk, dv, r.reshape(HEADS))
 
 
 def solution(mesh):

time: 144 us -> 115 us (0.80)
  the two profiles are of different devices: /device:TPU:56 before, /device:TPU:82 now
where the time goes in v2:
time: 115 us
  Pallas kernels  114 us (99%)
    pallas_call x1, Pallas kernels, body(): pl.pallas_call(kernel, out_shape=[jax.ShapeDtypeStruct(shape, bf16), jax....  112 us
    pallas_call x1, Pallas kernels, body(): pl.pallas_call(hand_over, out_shape=[jax.ShapeDtypeStruct(shape, bf16)] *...  2.36 us

profile of v2, /device:TPU:82, one launch (start us, length us, event | category | flops | bytes accessed | tf_op | source)
XLA Modules:
  0.0 114.9 jit_solution(16465860908488690082)
XLA Ops:
  0.6 111.9 %shard_map.102 = (bf16[1,128,2560]{2,1,0:T(8,128)(2,1)}, bf16[1,128,2560]{2,1,0:T(8,128)(2,1)}, bf16[1,128,2560]{2,1,0:T(8,128)(2,1)}, f32[1,20]{1,0:T(1,128)}) custom-call(f32[1,20]{1,0:T(1,128)} %bitcast.4, s32[1,20]{1,0:T(1,128)} %bitcast.5, bf16[1,128,2560]{2,1,0:T(8,128)(2,1)} %q_ref.1, bf16[1,128,2560]{2,1,0:T(8,128)(2,1)} %k_ref.1, ...), custom_call_target="tpu_custom_call" | custom-call | flops 7000000000 | bytes 5000000 | tf_op jit(solution)/shard_map/pallas_call | solution.py:383
  112.5 2.4 %shard_map.103 = (bf16[1,128,2560]{2,1,0:T(8,128)(2,1)}, bf16[1,128,2560]{2,1,0:T(8,128)(2,1)}, bf16[1,128,2560]{2,1,0:T(8,128)(2,1)}, f32[1,20]{1,0:T(1,128)}) custom-call(bf16[1,128,2560]{2,1,0:T(8,128)(2,1)} %get-tuple-element.12.dq_in, bf16[1,128,2560]{2,1,0:T(8,128)(2,1)} %get-tuple-element.13.dk_in, bf16[1,128,2560]{2,1,0:T(8,128)(2,1)} %get-tuple-element.14.dv_in, ...), custom_call_target="tpu_custom_call" | custom-call | tf_op jit(solution)/shard_map/pallas_call | solution.py:432

commit v3 on v2

--- a/solution.py
+++ b/solution.py
@@ -39,7 +39,7 @@
     dq_out, dk_out, dv_out, r_out,
     qb, kb, vb, gb, msb, kx, kt, s_buf, o_buf, ds_buf, dk_acc, dv_acc,
     dqs, dks, dvs, rmine, rb, rrow, rother,
-    in_send, in_recv, gf_send, gf_recv, ms_send, ms_recv, out_send, out_recv,
+    in_send, in_recv, q_recv, gf_send, gf_recv, ms_send, ms_recv, out_send, out_recv,
     rp_send, rp_recv, rb_send, rb_recv,
 ):
     me = lax.axis_index("ctx")
@@ -104,14 +104,17 @@
         rows = pl.ds(pl.multiple_of(step * HALF, HALF), HALF)
         send_pairs(h, ((g_ref.at[rows, columns(h)], gb.at[slot, me, step], in_recv.at[slot, 3]),))
 
-    def send_qkv(h):
+    def send_kv(h):
         slot = h // 16
         cols = columns(h)
         send_pairs(h, (
             (k_ref.at[0, :, cols], kb.at[slot, my_rows], in_recv.at[slot, 0]),
             (v_ref.at[0, :, cols], vb.at[slot, my_rows], in_recv.at[slot, 1]),
-            (q_ref.at[0, :, cols], qb.at[slot, my_rows], in_recv.at[slot, 2]),
         ))
+
+    def send_q(h):
+        slot = h // 16
+        send_pairs(h, ((q_ref.at[0, :, columns(h)], qb.at[slot, my_rows], q_recv.at[slot, me // 4]),))
 
     def loop(send, first, count, start):
         def one(j, _):
@@ -122,10 +125,13 @@
 
     loop(send_g, 0, 8, z)
     loop(send_g, 16, 4, z // 2)
-    loop(send_qkv, 0, 8, z)
+    loop(send_kv, 0, 8, z)
+    loop(send_q, 0, 8, z)
     loop(send_g, 8, 8, z)
-    loop(send_qkv, 16, 4, z // 2)
-    loop(send_qkv, 8, 8, z)
+    loop(send_kv, 16, 4, z // 2)
+    loop(send_q, 16, 4, z // 2)
+    loop(send_kv, 8, 8, z)
+    loop(send_q, 8, 8, z)
 
     def forward_g(slot):
         return pltpu.make_async_remote_copy(
@@ -169,7 +175,7 @@
         h = jnp.where(slot == 0, first_head, second_head)
         coef = jnp.sum(jnp.where(head_lane == h, coef_row, 0.0), axis=1, keepdims=True)
         cols = columns(h)
-        for a, buf in enumerate((kb, vb, qb)):
+        for a, buf in enumerate((kb, vb)):
             pltpu.make_async_copy(buf.at[slot], buf.at[slot], in_recv.at[slot, a]).wait()
         forward_g(slot).wait_recv()
 
@@ -200,6 +206,8 @@
 
         def unit(b, r_sum):
             q_rows = pl.ds(pl.multiple_of(b * BQ, BQ), BQ)
+            q_in = qb.at[slot, q_rows]
+            pltpu.make_async_copy(q_in, q_in, q_recv.at[slot, b]).wait()
             g_blk = gb[slot, pl.ds(b * (BQ // ROWS), BQ // ROWS)].reshape(BQ, DH)
             q_ext = jnp.concatenate([qb[slot, q_rows, :], ones], axis=1)
 
@@ -275,6 +283,7 @@
                 return 0
 
             def finish(t, _):
+                t = (t // 4) * 4 + (t + me) % 4
                 rows = pl.ds(pl.multiple_of(t * ROWS, ROWS), ROWS)
                 dks[slot, rows, :] = dk_acc[rows, :].astype(jnp.bfloat16)
                 dvs[slot, rows, :] = dv_acc[rows, :].astype(jnp.bfloat16)
@@ -354,26 +363,6 @@
         pltpu.make_async_copy(out, out, out_recv.at[a]).wait()
 
 
-def hand_over(
-    dq_in, dk_in, dv_in, r_in, dq_out, dk_out, dv_out, r_out, held, r_held, sems_in, sems_out,
-):
-    into, onward = [pltpu.make_async_copy(r_in, r_held, sems_in.at[0])], []
-    onward.append(pltpu.make_async_copy(r_held, r_out, sems_out.at[0]))
-    for a, (src, dst) in enumerate(((dq_in, dq_out), (dk_in, dk_out), (dv_in, dv_out))):
-        for i in range(2):
-            rows = pl.ds(i * HALF, HALF)
-            n = 1 + 2 * a + i
-            into.append(pltpu.make_async_copy(src.at[0, rows], held.at[a, rows], sems_in.at[n]))
-            onward.append(pltpu.make_async_copy(held.at[a, rows], dst.at[0, rows], sems_out.at[n]))
-    for copy in into:
-        copy.start()
-    for copy, after in zip(into, onward):
-        copy.wait()
-        after.start()
-    for copy in onward:
-        copy.wait()
-
-
 def body(queries, keys, values, cotangent, merge_sizes, router_logits, gate_plan):
     shape = queries.shape
     bf16, f32 = jnp.bfloat16, jnp.float32
@@ -383,13 +372,13 @@
     dq, dk, dv, r = pl.pallas_call(
         kernel,
         out_shape=[
-            jax.ShapeDtypeStruct(shape, bf16),
-            jax.ShapeDtypeStruct(shape, bf16),
-            jax.ShapeDtypeStruct(shape, bf16),
-            jax.ShapeDtypeStruct((1, HEADS), f32),
+            pltpu.VMEM(shape, bf16),
+            pltpu.VMEM(shape, bf16),
+            pltpu.VMEM(shape, bf16),
+            pltpu.VMEM((1, HEADS), f32),
         ],
         in_specs=[whole, whole] + [anywhere] * 5,
-        out_specs=[anywhere] * 3 + [whole],
+        out_specs=[whole] * 4,
         scratch_shapes=[
             pltpu.VMEM((2, TOK, DH), bf16),
             pltpu.VMEM((2, TOK, DH), bf16),
@@ -412,6 +401,7 @@
             pltpu.VMEM((1, DH), f32),
             dma((HEADS,)),
             dma((2, 4)),
+            dma((2, UNITS)),
             dma((2,)), dma((2,)),
             dma, dma,
             dma((2, 3)),
@@ -429,17 +419,6 @@
         router_logits.reshape(1, HEADS), gate_plan.reshape(1, HEADS),
         queries, keys, values, cotangent, merge_sizes.reshape(1, ROWS),
     )
-    dq, dk, dv, r = pl.pallas_call(
-        hand_over,
-        out_shape=[jax.ShapeDtypeStruct(shape, bf16)] * 3
-        + [jax.ShapeDtypeStruct((1, HEADS), f32)],
-        in_specs=[anywhere] * 4,
-        out_specs=[anywhere] * 4,
-        scratch_shapes=[
-            pltpu.VMEM((3,) + shape[1:], bf16), pltpu.VMEM((1, HEADS), f32), dma((7,)), dma((7,)),
-        ],
-        compiler_params=pltpu.CompilerParams(vmem_limit_bytes=60 * 1024 * 1024),
-    )(dq, dk, dv, r)
     return (dq, dk, dv, r.reshape(HEADS))
 
 

time: 115 us -> 112 us (0.974)
  the two profiles are of different devices: /device:TPU:82 before, /device:TPU:56 now
where the time goes in v3:
time: 112 us
  Pallas kernels  108 us (96%)
  local copies, waits for them, and re-layouts  3.02 us (3%)
    pallas_call x1, Pallas kernels, body(): pl.pallas_call(kernel, out_shape=[pltpu.VMEM(shape, bf16), pltpu.VMEM(sha...  108 us
    unnamed x4, local copies, waits for them, and re-layouts  3.02 us

profile of v3, /device:TPU:56, one launch (start us, length us, event | category | flops | bytes accessed | tf_op | source)
XLA Modules:
  0.0 111.8 jit_solution(4437346952141285607)
XLA Ops:
  0.6 108.1 %shard_map.102 = (bf16[1,128,2560]{2,1,0:T(8,128)(2,1)S(1)}, bf16[1,128,2560]{2,1,0:T(8,128)(2,1)S(1)}, bf16[1,128,2560]{2,1,0:T(8,128)(2,1)S(1)}, f32[1,20]{1,0:T(1,128)S(1)}) custom-call(f32[1,20]{1,0:T(1,128)} %bitcast.5, s32[1,20]{1,0:T(1,128)} %bitcast.6, bf16[1,128,2560]{2,1,0:T(8,128)(2,1)} %q_ref.1, bf16[1,128,2560]{2,1,0:T(8,128)(2,1)} %k_ref.1, ...), custom_call_target="tpu_custom_call" | custom-call | flops 7000000000 | bytes 5000000 | tf_op jit(solution)/shard_map/pallas_call | solution.py:372
  108.7 0.8 copy.15
  109.6 0.5 copy.18
  110.1 0.8 copy.16
  110.9 0.8 copy.17

commit v4 on v3

--- a/solution.py
+++ b/solution.py
@@ -35,12 +35,12 @@
 
 
 def kernel(
-    logit_ref, gate_ref, q_ref, k_ref, v_ref, g_ref, ms_ref,
+    logit_in, gate_in, q_ref, k_ref, v_ref, g_ref, ms_ref,
     dq_out, dk_out, dv_out, r_out,
     qb, kb, vb, gb, msb, kx, kt, s_buf, o_buf, ds_buf, dk_acc, dv_acc,
-    dqs, dks, dvs, rmine, rb, rrow, rother,
+    dqs, dks, dvs, rmine, rb, rrow, rother, logit_ref, gate_ref,
     in_send, in_recv, q_recv, gf_send, gf_recv, ms_send, ms_recv, out_send, out_recv,
-    rp_send, rp_recv, rb_send, rb_recv,
+    rp_send, rp_recv, rb_send, rb_recv, small_sem,
 ):
     me = lax.axis_index("ctx")
     step = lax.axis_index("step")
@@ -63,6 +63,12 @@
 
     lax.fori_loop(1, NDEV, greet, 0)
     pl.semaphore_signal(barrier, inc=1, device_id={"step": 1 - step}, device_id_type=MESH)
+    small = (
+        pltpu.make_async_copy(logit_in, logit_ref, small_sem.at[0]),
+        pltpu.make_async_copy(gate_in, gate_ref, small_sem.at[1]),
+    )
+    for copy in small:
+        copy.start()
     pl.semaphore_wait(barrier, NDEV)
 
     my_rows = pl.ds(pl.multiple_of(me * ROWS, ROWS), ROWS)
@@ -166,6 +172,8 @@
 
     lax.fori_loop(0, n_slots, pass_g_on, 0)
 
+    for copy in small:
+        copy.wait()
     beta = jnp.where(gate_ref[...] == 1, jax.nn.sigmoid(logit_ref[...]), 1.0)
     coef_row = jnp.where(step == 1, beta, 1.0 - beta)
     head_lane = lax.broadcasted_iota(jnp.int32, (1, HEADS), 1)
@@ -361,6 +369,20 @@
     r_out[...] = beta * (1.0 - beta) * total[:, :HEADS] * (1.0 / math.sqrt(TOK))
     for a, out in enumerate((dq_out, dk_out, dv_out)):
         pltpu.make_async_copy(out, out, out_recv.at[a]).wait()
+
+
+def hand_over(dq_in, dk_in, dv_in, r_in, dq_out, dk_out, dv_out, r_out, sems):
+    copies = [pltpu.make_async_copy(r_in, r_out, sems.at[0])]
+    for a, (src, dst) in enumerate(((dq_in, dq_out), (dk_in, dk_out), (dv_in, dv_out))):
+        for i in range(2):
+            rows = pl.ds(i * HALF, HALF)
+            copies.append(
+                pltpu.make_async_copy(src.at[0, rows], dst.at[0, rows], sems.at[1 + 2 * a + i])
+            )
+    for copy in copies:
+        copy.start()
+    for copy in copies:
+        copy.wait()
 
 
 def body(queries, keys, values, cotangent, merge_sizes, router_logits, gate_plan):
@@ -377,7 +399,7 @@
             pltpu.VMEM(shape, bf16),
             pltpu.VMEM((1, HEADS), f32),
         ],
-        in_specs=[whole, whole] + [anywhere] * 5,
+        in_specs=[anywhere] * 7,
         out_specs=[whole] * 4,
         scratch_shapes=[
             pltpu.VMEM((2, TOK, DH), bf16),
@@ -399,6 +421,8 @@
             pltpu.VMEM((HEADS, 1, DH), f32),
             pltpu.VMEM((1, DH), f32),
             pltpu.VMEM((1, DH), f32),
+            pltpu.VMEM((1, HEADS), f32),
+            pltpu.VMEM((1, HEADS), jnp.int32),
             dma((HEADS,)),
             dma((2, 4)),
             dma((2, UNITS)),
@@ -408,6 +432,7 @@
             dma((3,)),
             dma, dma,
             dma((2,)), dma,
+            dma((2,)),
         ],
         compiler_params=pltpu.CompilerParams(
             collective_id=0, has_side_effects=True, vmem_limit_bytes=60 * 1024 * 1024
@@ -419,6 +444,16 @@
         router_logits.reshape(1, HEADS), gate_plan.reshape(1, HEADS),
         queries, keys, values, cotangent, merge_sizes.reshape(1, ROWS),
     )
+    held = [pltpu.with_memory_space_constraint(a, pltpu.VMEM) for a in (dq, dk, dv, r)]
+    dq, dk, dv, r = pl.pallas_call(
+        hand_over,
+        out_shape=[jax.ShapeDtypeStruct(shape, bf16)] * 3
+        + [jax.ShapeDtypeStruct((1, HEADS), f32)],
+        in_specs=[whole] * 4,
+        out_specs=[anywhere] * 4,
+        scratch_shapes=[dma((7,))],
+        compiler_params=pltpu.CompilerParams(vmem_limit_bytes=60 * 1024 * 1024),
+    )(*held)
     return (dq, dk, dv, r.reshape(HEADS))
 
 

time: 112 us -> 110 us (0.982)
  local copies, waits for them, and re-layouts: 3.02 us -> 0 us
    unnamed x4 -> x0, local copies, waits for them, and re-layouts: 3.02 us -> none
    pallas_call x0 -> x1, Pallas kernels: none -> 1.33 us  [body(): pl.pallas_call(hand_over, out_shape=[jax.ShapeDtypeStruct(shape, bf16)] *...]
where the time goes in v4:
time: 110 us
  Pallas kernels  109 us (99%)
    pallas_call x1, Pallas kernels, body(): pl.pallas_call(kernel, out_shape=[pltpu.VMEM(shape, bf16), pltpu.VMEM(sha...  108 us

profile of v4, /device:TPU:56, one launch (start us, length us, event | category | flops | bytes accessed | tf_op | source)
XLA Modules:
  0.0 109.5 jit_solution(3751469380050316221)
XLA Ops:
  0.6 107.6 %shard_map.102 = (bf16[1,128,2560]{2,1,0:T(8,128)(2,1)S(1)}, bf16[1,128,2560]{2,1,0:T(8,128)(2,1)S(1)}, bf16[1,128,2560]{2,1,0:T(8,128)(2,1)S(1)}, f32[1,20]{1,0:T(1,128)S(1)}) custom-call(f32[1,20]{1,0:T(1,128)} %bitcast.4, s32[1,20]{1,0:T(1,128)} %bitcast.5, bf16[1,128,2560]{2,1,0:T(8,128)(2,1)} %q_ref.1, bf16[1,128,2560]{2,1,0:T(8,128)(2,1)} %k_ref.1, ...), custom_call_target="tpu_custom_call" | custom-call | flops 7000000000 | bytes 5000000 | tf_op jit(solution)/shard_map/pallas_call | solution.py:394
  108.2 1.3 %shard_map.103 = (bf16[1,128,2560]{2,1,0:T(8,128)(2,1)}, bf16[1,128,2560]{2,1,0:T(8,128)(2,1)}, bf16[1,128,2560]{2,1,0:T(8,128)(2,1)}, f32[1,20]{1,0:T(1,128)}) custom-call(bf16[1,128,2560]{2,1,0:T(8,128)(2,1)S(1)} %get-tuple-element.12.dq_in, bf16[1,128,2560]{2,1,0:T(8,128)(2,1)S(1)} %get-tuple-element.13.dk_in, ...), custom_call_target="tpu_custom_call" | custom-call | tf_op jit(solution)/shard_map/pallas_call | solution.py:448

commit v5 on v4

--- a/solution.py
+++ b/solution.py
@@ -300,6 +300,8 @@
                 return 0
 
             def pass3_send(c, _):
+                far_first = jnp.logical_and(slot == 1, z == 0)
+                c = jnp.where(far_first, TOK // CK - 1 - c, c)
                 pass3(c, 0)
 
                 @pl.when(b == UNITS - 1)

time: 110 us -> 110 us (level)
  no operation moved by 1% of the time
where the time goes in v5:
time: 110 us
  Pallas kernels  109 us (99%)
    pallas_call x1, Pallas kernels, body(): pl.pallas_call(kernel, out_shape=[pltpu.VMEM(shape, bf16), pltpu.VMEM(sha...  108 us

profile of v5, /device:TPU:56, one launch (start us, length us, event | category | flops | bytes accessed | tf_op | source)
XLA Modules:
  0.0 109.6 jit_solution(10282245504582396547)
XLA Ops:
  0.6 107.6 %shard_map.102 = (bf16[1,128,2560]{2,1,0:T(8,128)(2,1)S(1)}, bf16[1,128,2560]{2,1,0:T(8,128)(2,1)S(1)}, bf16[1,128,2560]{2,1,0:T(8,128)(2,1)S(1)}, f32[1,20]{1,0:T(1,128)S(1)}) custom-call(f32[1,20]{1,0:T(1,128)} %bitcast.4, s32[1,20]{1,0:T(1,128)} %bitcast.5, bf16[1,128,2560]{2,1,0:T(8,128)(2,1)} %q_ref.1, bf16[1,128,2560]{2,1,0:T(8,128)(2,1)} %k_ref.1, ...), custom_call_target="tpu_custom_call" | custom-call | flops 7000000000 | bytes 5000000 | tf_op jit(solution)/shard_map/pallas_call | solution.py:396
  108.2 1.3 %shard_map.103 = (bf16[1,128,2560]{2,1,0:T(8,128)(2,1)}, bf16[1,128,2560]{2,1,0:T(8,128)(2,1)}, bf16[1,128,2560]{2,1,0:T(8,128)(2,1)}, f32[1,20]{1,0:T(1,128)}) custom-call(bf16[1,128,2560]{2,1,0:T(8,128)(2,1)S(1)} %get-tuple-element.12.dq_in, bf16[1,128,2560]{2,1,0:T(8,128)(2,1)S(1)} %get-tuple-element.13.dk_in, ...), custom_call_target="tpu_custom_call" | custom-call | tf_op jit(solution)/shard_map/pallas_call | solution.py:450
